TPU v7x, 32 devices: a whole 2x2x4 slice. The times are simulated.
32 devices in a mesh: groups: 2 (over y), section: 4 (over z), tp: 4 (over x, core).
Axes of the slice: x: 2, y: 2, z: 4, core: 2. Of those that a mesh axis runs over, the one named last changes fastest.
Arguments:
- tokens: bfloat16 [8192, 8192], P(('groups', 'section'), 'tp'), parts along dimension 0
- norm_gain: bfloat16 [8192], P('tp'), may hold values from 0.29882812 to 3
- kv_weight: bfloat16 [8192, 8, 256], P('tp'), may hold values from -0.015625 to 0.015625
- block_owner: int32 [64, 1], P('groups'), parts along dimension 0, may hold values from 0 to 3; in each aligned block of 8 rows (0 to 7, 8 to 15, ...) at most 4 rows name the same one
- resident_cache: bfloat16 [8, 256, 128, 256], P('tp', ('groups', 'section')), parts along dimension 1, may hold values from -5 to 5
- page_table: int32 [256, 8], P(('groups', 'section')), parts along dimension 0, may hold values from 0 to 47, as said below
- context_len: int32 [256], P(('groups', 'section')), parts along dimension 0, may hold values from 2 to 1024
- decode_query: bfloat16 [8, 256, 8, 128], P('tp', ('groups', 'section')), parts along dimension 1, may hold values from -30 to 30
- new_kv: bfloat16 [8, 256, 256], P('tp', ('groups', 'section')), parts along dimension 1, may hold values from -5 to 5
Outputs:
- decoded: float32 [8, 256, 8, 128], P('tp', ('groups', 'section')), parts along dimension 1
There are 2 independent parts, one for each index of `groups`. A program takes and returns all parts, laid end to end along the dimension named above; an argument that names none is the same for every part. Nothing has to cross between parts.
Inputs may be any that keep to these rules, and one draw needn't show every extreme that they name: `block_owner`: within the 8 blocks of one prefill device no owner is named more than 4 times, a bound that some block reaches. `page_table`: column 0 of every request names a resident page (below 32), a different one for each request of one owner; the other columns name any page.
All inputs are finite; a program needn't handle non-finite values.
Results may differ from a plain program's by a relative error of at most 0.0016.
Values may be sent and summed in bfloat16 or wider, within the bound.
A program may use at most 192 MiB of HBM per device.

v0:
```python
import math

import jax
import jax.numpy as jnp
from jax import lax
from jax.sharding import PartitionSpec as P

D = 8192


EPSILON = 1e-05


def block_ranks(owner_grid):
    blocks_dev = owner_grid.shape[1]
    same_owner = owner_grid[:, :, None] == owner_grid[:, None, :]
    positions = jnp.arange(blocks_dev, dtype=jnp.int32)
    earlier = positions[None, :] < positions[:, None]
    return jnp.sum((same_owner & earlier[None]).astype(jnp.int32), axis=2)


def attend(page_pool, table, lengths, queries, fresh):
    heads_dev, requests, group_size, head_dim = queries.shape
    length = table.shape[1] * page_pool.shape[2]
    gathered = page_pool[:, table].reshape(heads_dev, requests, length, 2 * head_dim)
    cache_keys = gathered[..., :head_dim]
    cache_values = gathered[..., head_dim:]
    score_scale = 1.0 / math.sqrt(head_dim)
    scores = (
        jnp.einsum("hrgd,hrld->hrgl", queries, cache_keys, preferred_element_type=jnp.float32)
        * score_scale
    )
    own_score = (
        jnp.einsum(
            "hrgd,hrd->hrg", queries, fresh[..., :head_dim], preferred_element_type=jnp.float32
        )
        * score_scale
    )
    positions = jnp.arange(length, dtype=jnp.int32)
    live_mask = (positions[None, :] < lengths[:, None])[None, :, None, :]
    masked = jnp.where(live_mask, scores, jnp.float32(-1e30))
    row_max = jnp.maximum(jnp.max(masked, axis=3), own_score)
    weights = jnp.where(live_mask, jnp.exp(masked - row_max[..., None]), jnp.float32(0.0))
    own_weight = jnp.exp(own_score - row_max)
    denominator = jnp.sum(weights, axis=3) + own_weight
    weights_low = weights.astype(jnp.bfloat16)
    own_low = lax.optimization_barrier(own_weight.astype(jnp.bfloat16)).astype(jnp.float32)
    mixed = jnp.einsum(
        "hrgl,hrld->hrgd", weights_low, cache_values, preferred_element_type=jnp.float32
    )
    mixed = mixed + own_low[..., None] * fresh[:, :, None, head_dim:].astype(jnp.float32)
    return mixed / denominator[..., None]


def per_device(
    tokens,
    norm_gain,
    kv_weight,
    block_owner,
    resident_cache,
    page_table,
    context_len,
    decode_query,
    new_kv,
):
    heads_dev = resident_cache.shape[0]
    block_rows = resident_cache.shape[2]
    lanes = resident_cache.shape[3]
    blocks_dev = tokens.shape[0] // block_rows
    sections = lax.axis_size("section")
    slots_peer = 2 * ((blocks_dev + sections - 1) // sections)
    widened = tokens.astype(jnp.float32)
    local_squares = jnp.sum(widened * widened, axis=1)
    normed = (widened * norm_gain.astype(jnp.float32)[None, :]).astype(jnp.bfloat16)
    squares = lax.psum(local_squares, "tp")
    summed = lax.psum_scatter(
        jnp.einsum("td,dhc->htc", normed, kv_weight, preferred_element_type=jnp.float32).astype(
            jnp.bfloat16
        ),
        "tp",
        scatter_dimension=0,
        tiled=True,
    ).astype(jnp.float32)
    keyval = (summed * lax.rsqrt(squares / D + EPSILON)[None, :, None]).astype(jnp.bfloat16)
    blocks = keyval.reshape(heads_dev, blocks_dev, block_rows, lanes)
    owner_flat = block_owner[:, 0]
    rank_flat = block_ranks(owner_flat.reshape(sections, blocks_dev)).reshape(-1)
    owner_self = lax.axis_index("section")
    slot_ids = jnp.arange(sections * slots_peer, dtype=jnp.int32)
    shard_rows = lax.all_gather(blocks, "section", axis=1, tiled=True)
    row_count = shard_rows.shape[1]
    global_ids = jnp.arange(row_count, dtype=jnp.int32)
    target = global_ids // blocks_dev * slots_peer + rank_flat
    matches = (slot_ids[:, None] == target[None, :]) & (owner_flat[None, :] == owner_self)
    received = jnp.einsum(
        "si,hibc->hsbc",
        matches.astype(jnp.bfloat16),
        shard_rows,
        preferred_element_type=jnp.float32,
    ).astype(jnp.bfloat16)
    page_pool = jnp.concatenate([resident_cache, received], axis=1)
    return attend(page_pool, page_table, context_len, decode_query, new_kv)


def solution(mesh):
    return jax.shard_map(
        per_device,
        mesh=mesh,
        in_specs=(
            P(("groups", "section"), "tp"),
            P("tp"),
            P("tp", None, None),
            P("groups", None),
            P("tp", ("groups", "section"), None, None),
            P(("groups", "section"), None),
            P(("groups", "section")),
            P("tp", ("groups", "section"), None, None),
            P("tp", ("groups", "section"), None),
        ),
        out_specs=P("tp", ("groups", "section"), None, None),
        check_vma=False,
    )
```

profile of v0, /device:TPU:0, one launch (start us, length us, event | category | flops | bytes accessed | tf_op | source)
XLA Modules:
  0.0 222.8 jit_solution(3781500358210486599)
XLA Ops:
  6.5 0.7 convert_element_type.45
  7.3 13.9 %convert_bitcast_fusion = bf16[8,1024,256]{2,1,0:T(8,128)(2,1)} fusion(bf16[2048,8,256]{2,1,0:T(8,128)(2,1)} %param.11, bf16[1024,2048]{1,0:T(8,128)(2,1)} %param.9, f32[2048]{0:T(1024)S(1)} %convert_element_type.45), kind=kOutput, calls=%fused_computation.13 | convolution fusion | flops 8598323200 | bytes 16785408 | tf_op jit(solution)/shard_map/td,dhc->htc/dot_general | solution.py:77
  21.1 0.0 reduce-scatter.2.cloned.1.call-update
  21.2 0.0 copy-start.5
  21.2 0.0 copy-start.3
  21.2 0.0 copy-start.4
  21.2 0.0 copy-start.2
  21.2 0.0 all-gather.2.cloned.1.call-start
  21.3 3.1 %fusion.5 = f32[1024]{0:T(1024)S(1)} fusion(bf16[1024,2048]{1,0:T(8,128)(2,1)} %param.9), kind=kLoop, calls=%fused_computation.8 | loop fusion | flops 6290432 | bytes 4198400 | tf_op jit(solution)/shard_map/reduce_sum | solution.py:73
  24.3 8.3 %psum.7 = f32[1024]{0:T(1024)S(1)} all-reduce(f32[1024]{0:T(1024)S(1)} %fusion.5), channel_id=1, replica_groups=mesh['groups'=2,'section'=4,'tp'=4] {'tp'}, use_global_device_ids=true, to_apply=%region_2.0 | all-reduce | flops 1024 | bytes 8192 | tf_op jit(solution)/shard_map/psum | solution.py:75
  32.7 35.8 %reduce-scatter.2.cloned.1.call-done = bf16[2,1024,256]{2,1,0:T(8,128)(2,1)} async-done(((bf16[8,1024,256]{2,1,0:T(8,128)(2,1)}), bf16[2,1024,256]{2,1,0:T(8,128)(2,1)}) %reduce-scatter.2.cloned.1.call-update) | async-done | bytes 1048592 | tf_op jit(solution)/shard_map/reduce_scatter | solution.py:76
  68.5 1.5 multiply_convert_fusion
  70.1 1.6 copy.20
  71.6 0.0 all-gather.2.cloned.1.call-update
  71.7 0.5 broadcast.74
  72.2 0.7 reduce.3
  72.8 0.1 eq.43
  72.9 0.2 convert_reduce_fusion
  73.1 0.1 reshape.77
  73.2 0.1 copy.22
  73.3 0.1 reshape.81
  73.5 0.1 iota_compare_fusion
  73.6 0.2 fusion.32
  73.8 78.6 %all-gather.2.cloned.1.call-done = bf16[2,32,128,256]{3,1,2,0:T(8,128)(2,1)} async-done(((bf16[2,8,128,256]{3,1,2,0:T(8,128)(2,1)}), bf16[2,32,128,256]{3,1,2,0:T(8,128)(2,1)}) %all-gather.2.cloned.1.call-update) | async-done | bytes 4194320 | tf_op jit(solution)/shard_map/all_gather | solution.py:90
  152.4 3.0 %convert_bitcast_fusion.1 = bf16[2,16,128,256]{3,1,2,0:T(8,128)(2,1)S(1)} fusion(bf16[2,32,128,256]{3,1,2,0:T(8,128)(2,1)} %all-gather.2.cloned.1.call-done, s32[32]{0:T(128)S(1)} %fusion.42, pred[32]{0:T(512)(128)(4,1)S(1)} %compare_bitcast_fusion), kind=kOutput, calls=%fused_computation.20 | convolution fusion | flops 68158464 | bytes 6291616 | tf_op jit(solution)/shard_map/si,hibc->hsbc/dot_general | solution.py:95
  155.4 0.7 copy.21
  156.2 3.1 %pad_maximum_fusion = bf16[2,48,128,256]{3,2,1,0:T(8,128)(2,1)} fusion(bf16[2,16,128,256]{3,2,1,0:T(8,128)(2,1)S(1)} %copy.21, bf16[2,32,128,256]{3,2,1,0:T(8,128)(2,1)S(1)} %copy-done.1), kind=kLoop, calls=%fused_computation.11 | loop fusion | flops 3145728 | bytes 12582912 | tf_op jit(solution)/shard_map/concatenate | solution.py:101
  159.3 16.6 %gather_fusion = bf16[256,2,128,256]{3,2,1,0:T(8,128)(2,1)} fusion(bf16[2,48,128,256]{3,2,1,0:T(8,128)(2,1)} %pad_maximum_fusion, s32[1024]{0:T(1024)S(1)} %pad_clamp_fusion), kind=kCustom, calls=%fused_computation | custom fusion | bytes 67109888 | tf_op jit(solution)/shard_map/gather | solution.py:25
  175.9 22.9 %copy.23 = bf16[32,8,2,128,256]{4,3,1,0,2:T(8,128)(2,1)} copy(bf16[32,8,2,128,256]{4,3,2,1,0:T(8,128)(2,1)} %bitcast.41) | data formatting | bytes 67108864 | tf_op jit(solution)/shard_map/gather | solution.py:25
  198.9 8.1 %bitcast_reduce_fusion = (f32[2,32,8]{2,1,0:T(8,128)S(1)}, f32[2,32,1024,8]{2,3,1,0:T(8,128)S(1)}) fusion(pred[32,1024]{1,0:T(8,128)(4,1)S(1)} %iota_compare_fusion, bf16[2,32,8,128]{3,2,1,0:T(8,128)(2,1)S(1)} %copy-done, bf16[2,32,1024,256]{3,2,1,0:T(8,128)(2,1)} %bitcast.42), kind=kOutput, calls=%fused_computation.16 | convolution fusion | flops 135790080 | bytes 19040256 | tf_op jit(solution)/shard_map/hrgd,hrld->hrgl/dot_general | solution.py:30
  207.0 0.9 fusion.17
  208.0 8.0 %fusion.22 = f32[2,32,8,128]{3,2,1,0:T(8,128)} fusion(bf16[2,32,1024,256]{3,2,1,0:T(8,128)(2,1)} %bitcast.43, f32[2,32,1024,8]{2,3,1,0:T(8,128)S(1)} %get-tuple-element.10, f32[2,32,8]{2,1,0:T(8,128)S(1)} %multiply_maximum_fusion, pred[32,1024]{1,0:T(8,128)(4,1)S(1)} %iota_compare_fusion, f32[2,32,8]{2,1,0:T(8,128)S(1)} %get-tuple-element.6, ...), kind=kOutput, calls=%fused_computation.25 | convolution fusion | flops 137035776 | bytes 19333120 | tf_op jit(solution)/shard_map/hrgl,hrld->hrgd/dot_general | solution.py:48
  (19 shorter events, 0.1 us)
Async XLA Ops:
  6.5 67.0 %copy-start = (bf16[2,32,8,128]{3,2,1,0:T(8,128)(2,1)S(1)}, bf16[2,32,8,128]{3,2,1,0:T(8,128)(2,1)}, u32[]{:S(2)}) copy-start(bf16[2,32,8,128]{3,2,1,0:T(8,128)(2,1)} %param.16) | copy-start | bytes 393220
  6.5 62.0 %reduce-scatter.2.cloned.1.call-start = ((), (), s32[]{:S(2)}) async-start(), calls=%async_computation.1 | async-start | bytes 5242880 | tf_op jit(solution)/shard_map/reduce_scatter | solution.py:76
  21.2 51.0 %copy-start.5 = (s32[32,1]{0,1:T(1,128)S(1)}, s32[32,1]{0,1:T(1,128)}, u32[]{:S(2)}) copy-start(s32[32,1]{0,1:T(1,128)} %param.12) | copy-start | bytes 388
  21.2 52.1 %copy-start.3 = (s32[32,8]{0,1:T(8,128)S(1)}, s32[32,8]{0,1:T(8,128)}, u32[]{:S(2)}) copy-start(s32[32,8]{0,1:T(8,128)} %param.14) | copy-start | bytes 3076
  21.2 52.3 %copy-start.4 = (s32[32]{0:T(128)S(1)}, s32[32]{0:T(128)}, u32[]{:S(2)}) copy-start(s32[32]{0:T(128)} %param.15) | copy-start | bytes 388
  21.2 52.4 %copy-start.2 = (bf16[2,32,256]{2,1,0:T(8,128)(2,1)S(1)}, bf16[2,32,256]{2,1,0:T(8,128)(2,1)}, u32[]{:S(2)}) copy-start(bf16[2,32,256]{2,1,0:T(8,128)(2,1)} %param.17) | copy-start | bytes 98308
  21.2 131.2 %all-gather.2.cloned.1.call-start = ((), (), s32[]{:S(2)}) async-start(), calls=%async_computation.2 | async-start | bytes 5242880 | tf_op jit(solution)/shard_map/all_gather | solution.py:90
  152.4 3.8 %copy-start.1 = (bf16[2,32,128,256]{3,2,1,0:T(8,128)(2,1)S(1)}, bf16[2,32,128,256]{3,2,1,0:T(8,128)(2,1)}, u32[]{:S(2)}) copy-start(bf16[2,32,128,256]{3,2,1,0:T(8,128)(2,1)} %param.13) | copy-start | bytes 12582916
Sparse Core Ops, SparseCore 0:
  21.3 47.2 reduce-scatter.1
  71.8 80.5 all-gather.1
where the time goes:
time: 223 us
  waiting for transfers between devices  114 us (51%)
  local copies, waits for them, and re-layouts  42.8 us (19%)
  matrix products  33.2 us (15%)
  between operations  13.6 us (6%)
  other arithmetic  10.4 us (5%)
  blocking collectives  8.35 us (4%)
    all_gather x1, waiting for transfers between devices, per_device(): shard_rows = lax.all_gather(blocks, 'section', axis=1, tiled=True)  78.6 us
    gather x2, local copies, waits for them, and re-layouts, attend(): page_pool[:, table].reshape(heads_dev, requests, length, 2 * head_dim)  39.6 us
    reduce_scatter x1, waiting for transfers between devices, per_device(): lax.psum_scatter(jnp.einsum('td,dhc->htc', normed, kv_weight, preferred_e...  35.8 us
    dot_general x1, matrix products, per_device(): jnp.einsum('td,dhc->htc', normed, kv_weight, preferred_element_type=jnp.f...  13.9 us
    psum x1, blocking collectives, per_device(): squares = lax.psum(local_squares, 'tp')  8.35 us
    dot_general x1, matrix products, attend(): jnp.einsum('hrgd,hrld->hrgl', queries, cache_keys, preferred_element_type...  8.13 us
    dot_general x1, matrix products, attend(): jnp.einsum('hrgl,hrld->hrgd', weights_low, cache_values, preferred_elemen...  7.96 us
  transfers between devices with their start and end apart: 2, of which 2 were waited for; matrix products, arithmetic and copies ran while one was open for 2% of the time, Pallas kernels for 0%

commit v1 on v0

v1 whole, which is shorter than its diff:
```python
import functools
import math

import jax
import jax.numpy as jnp
from jax import lax
from jax.experimental import pallas as pl
from jax.experimental.pallas import tpu as pltpu
from jax.sharding import PartitionSpec as P

D = 8192


EPSILON = 1e-05
NEG = -1e30
GROUP = 4
MESH = pl.DeviceIdType.MESH


def block_ranks(owner_grid):
    blocks_dev = owner_grid.shape[1]
    same_owner = owner_grid[:, :, None] == owner_grid[:, None, :]
    positions = jnp.arange(blocks_dev, dtype=jnp.int32)
    earlier = positions[None, :] < positions[:, None]
    return jnp.sum((same_owner & earlier[None]).astype(jnp.int32), axis=2)


def page_counts(table, lengths, owner_flat, sections, pool, block, group_size):
    blocks_dev = owner_flat.shape[0] // sections
    slots_peer = 2 * ((blocks_dev + sections - 1) // sections)
    rank = block_ranks(owner_flat.reshape(sections, blocks_dev)).reshape(-1)
    ids = jnp.arange(owner_flat.shape[0], dtype=jnp.int32)
    placed = jnp.where(
        owner_flat == lax.axis_index("section"), pool + ids // blocks_dev * slots_peer + rank, -1
    )
    pages = jnp.concatenate([jnp.arange(pool, dtype=jnp.int32), placed])
    columns = jnp.repeat(table.T, group_size, axis=1)
    length = jnp.repeat(lengths, group_size)[None]
    begin = jnp.arange(columns.shape[0], dtype=jnp.int32)[:, None] * block
    whole = begin + block <= length
    partial = (begin < length) & ~whole
    same = pages[:, None, None] == columns[None]
    full = jnp.sum((same & whole[None]).astype(jnp.float32), axis=1)
    edge = jnp.sum((same & partial[None]).astype(jnp.float32), axis=1)
    rest = (length % block).astype(jnp.float32)
    zeros = length.astype(jnp.float32) - jnp.sum(full * block + edge * rest, axis=0, keepdims=True)
    misc = jnp.concatenate([rest, zeros, jnp.zeros((6, rest.shape[1]), jnp.float32)], axis=0)
    return full, edge, misc


def kernel(
    sections, tp, heads, block, chunk,
    part_ref, sq_ref, query_ref, cache_ref, fresh_ref, full_ref, edge_ref, aux_ref,
    out_ref,
    sib, cross_out, cross_in, sq_in, query_in, aux_in, kv, pages, scores, acc, res_acc,
    back_out, back_in, stat_out, stat_in, own_acc,
    sib_s, sib_r, cross_s, cross_r, sq_s, sq_r, query_s, query_r, aux_s, aux_r,
    back_s, back_r, stat_s, stat_r, page_s,
):
    me = lax.axis_index("section")
    t = lax.axis_index("tp")
    core, x = lax.rem(t, 2), lax.div(t, 2)
    chips = tp // 2
    rows = part_ref.shape[1]
    chunks = rows // chunk
    cols = query_ref.shape[1]
    dim = query_ref.shape[2]
    pool = cache_ref.shape[1]
    blocks_dev = rows // block
    scale = 1.0 / math.sqrt(dim)

    barrier = pltpu.get_barrier_semaphore()
    for d in range(1, tp):
        pl.semaphore_signal(
            barrier, inc=1, device_id={"tp": lax.rem(t + d, tp)}, device_id_type=MESH
        )
    for d in range(1, sections):
        pl.semaphore_signal(
            barrier, inc=1, device_id={"section": lax.rem(me + d, sections)}, device_id_type=MESH
        )
    pl.semaphore_wait(barrier, tp + sections - 2)

    def span(i):
        return pl.ds(pl.multiple_of(i * chunk, chunk), chunk)

    def sib_copy(d, i):
        group = lax.rem(x + d, chips) * 2 + 1 - core
        return pltpu.make_async_remote_copy(
            src_ref=part_ref.at[pl.ds(group * heads, heads), span(i)],
            dst_ref=sib.at[d, :, span(i)],
            send_sem=sib_s.at[d, i],
            recv_sem=sib_r.at[d, i],
            device_id={"tp": x * 2 + 1 - core},
            device_id_type=MESH,
        )

    def cross_copy(d, i):
        return pltpu.make_async_remote_copy(
            src_ref=cross_out.at[d - 1, :, span(i)],
            dst_ref=cross_in.at[d - 1, :, span(i)],
            send_sem=cross_s.at[d - 1, i],
            recv_sem=cross_r.at[d - 1, i],
            device_id={"tp": lax.rem(x + d, chips) * 2 + core},
            device_id_type=MESH,
        )

    def sq_copy(d):
        return pltpu.make_async_remote_copy(
            src_ref=sq_ref,
            dst_ref=sq_in.at[d - 1],
            send_sem=sq_s.at[d - 1],
            recv_sem=sq_r.at[d - 1],
            device_id={"tp": lax.rem(t + d, tp)},
            device_id_type=MESH,
        )

    def query_copy(d):
        return pltpu.make_async_remote_copy(
            src_ref=query_ref,
            dst_ref=query_in.at[d - 1],
            send_sem=query_s.at[d - 1],
            recv_sem=query_r.at[d - 1],
            device_id={"section": lax.rem(me + d, sections)},
            device_id_type=MESH,
        )

    def aux_copy(d):
        peer = lax.rem(me + d, sections)
        return pltpu.make_async_remote_copy(
            src_ref=aux_ref.at[peer],
            dst_ref=aux_in.at[d - 1],
            send_sem=aux_s.at[d - 1],
            recv_sem=aux_r.at[d - 1],
            device_id={"section": peer},
            device_id_type=MESH,
        )

    def back_copy(d):
        return pltpu.make_async_remote_copy(
            src_ref=back_out.at[d - 1],
            dst_ref=back_in.at[d - 1],
            send_sem=back_s.at[d - 1],
            recv_sem=back_r.at[d - 1],
            device_id={"section": lax.rem(me + sections - d, sections)},
            device_id_type=MESH,
        )

    def stat_copy(d):
        return pltpu.make_async_remote_copy(
            src_ref=stat_out.at[d - 1],
            dst_ref=stat_in.at[d - 1],
            send_sem=stat_s.at[d - 1],
            recv_sem=stat_r.at[d - 1],
            device_id={"section": lax.rem(me + sections - d, sections)},
            device_id_type=MESH,
        )

    def page_copy():
        return pltpu.make_async_copy(cache_ref, pages, page_s)

    for d in range(1, chips):
        for i in range(chunks):
            sib_copy(d, i).start()
    for d in range(1, tp):
        sq_copy(d).start()
    page_copy().start()
    for i in range(chunks):
        sib_copy(0, i).start()
    for d in range(1, sections):
        query_copy(d).start()
        aux_copy(d).start()

    for d in range(1, chips):
        group = lax.rem(x + d, chips) * 2 + core
        for i in range(chunks):
            sib_copy(d, i).wait_recv()
            mine = part_ref[pl.ds(group * heads, heads), span(i)]
            theirs = sib[d, :, span(i)]
            cross_out[d - 1, :, span(i)] = (
                mine.astype(jnp.float32) + theirs.astype(jnp.float32)
            ).astype(jnp.bfloat16)
            cross_copy(d, i).start()

    position = lax.broadcasted_iota(jnp.int32, (block, cols), 0).astype(jnp.float32)

    def attend(query, load, count_rows, rest, n_pages, extra=None, zeros=None):
        inside = position < rest

        def count(p):
            full, edge = count_rows(p)
            return full + jnp.where(inside, edge, 0.0)

        def first(step, top):
            base = step * GROUP
            for k in range(GROUP):
                keys = load(base + k)[:, :dim]
                s = lax.dot_general(
                    keys, query, (((1,), (1,)), ((), ())), preferred_element_type=jnp.float32
                ) * scale
                s = jnp.where(count(base + k) > 0, s, NEG)
                scores[pl.ds(pl.multiple_of((base + k) * block, block), block)] = s
                top = jnp.maximum(top, jnp.max(s.reshape(block // 8, 8, cols), axis=0))
            return top

        top = lax.fori_loop(0, n_pages // GROUP, first, jnp.full((8, cols), NEG, jnp.float32))
        top = jnp.max(top, axis=0, keepdims=True)
        if extra is not None:
            fresh = extra
            requests = fresh.shape[0]
            own = (
                lax.broadcasted_iota(jnp.int32, (requests, cols), 0) * (cols // requests)
            )
            column = lax.broadcasted_iota(jnp.int32, (requests, cols), 1)
            own = (column >= own) & (column < own + cols // requests)
            s_own = lax.dot_general(
                fresh[:, :dim], query, (((1,), (1,)), ((), ())), preferred_element_type=jnp.float32
            ) * scale
            s_own = jnp.where(own, s_own, NEG)
            top = jnp.maximum(top, jnp.max(s_own, axis=0, keepdims=True))
            top = jnp.maximum(top, jnp.where(zeros > 0, 0.0, NEG))
            w_own = jnp.where(own, jnp.exp(s_own - top), 0.0)
            acc[...] = lax.dot_general(
                fresh[:, dim:], w_own.astype(jnp.bfloat16), (((0,), (0,)), ((), ())),
                preferred_element_type=jnp.float32,
            )
            total = jnp.sum(w_own, axis=0, keepdims=True)
            total = total + jnp.where(zeros > 0, zeros * jnp.exp(0.0 - top), 0.0)
        else:
            acc[...] = jnp.zeros_like(acc)
            total = jnp.zeros((1, cols), jnp.float32)

        def second(step, total8):
            base = step * GROUP
            values, lows = [], []
            for k in range(GROUP):
                s = scores[pl.ds(pl.multiple_of((base + k) * block, block), block)]
                w = jnp.exp(s - top)
                c = count(base + k)
                total8 = total8 + jnp.sum((w * c).reshape(block // 8, 8, cols), axis=0)
                low = w.astype(jnp.bfloat16).astype(jnp.float32) * c
                lows.append(low.astype(jnp.bfloat16))
                values.append(load(base + k)[:, dim:])
            acc[...] += lax.dot_general(
                jnp.concatenate(values, axis=0), jnp.concatenate(lows, axis=0),
                (((0,), (0,)), ((), ())), preferred_element_type=jnp.float32,
            )
            return total8

        total8 = lax.fori_loop(0, n_pages // GROUP, second, jnp.zeros((8, cols), jnp.float32))
        return top, total + jnp.sum(total8, axis=0, keepdims=True)

    page_copy().wait()
    rest_own = aux_ref[0, 2 * blocks_dev : 2 * blocks_dev + 1, :]
    zeros_own = aux_ref[0, 2 * blocks_dev + 1 : 2 * blocks_dev + 2, :]
    res_stats = []
    for h in range(heads):
        stat = attend(
            query_ref[h],
            lambda p, h=h: pages[h, p],
            lambda p: (full_ref[pl.ds(p, 1), :], edge_ref[pl.ds(p, 1), :]),
            rest_own,
            pool,
            fresh_ref[h],
            zeros_own,
        )
        res_stats.append(stat)
        res_acc[h] = acc[...]

    for d in range(1, tp):
        sq_copy(d).wait_recv()
    squares = sq_ref[...]
    for d in range(1, tp):
        squares = squares + sq_in[d - 1]
    inverse = lax.rsqrt(squares / D + EPSILON)
    diagonal = lax.broadcasted_iota(jnp.int32, (block, block), 0) == lax.broadcasted_iota(
        jnp.int32, (block, block), 1
    )
    per_chunk = chunk // block
    for i in range(chunks):
        sib_copy(0, i).wait_recv()
        for d in range(1, chips):
            cross_copy(d, i).wait_recv()
        for k in range(per_chunk):
            j = i * per_chunk + k
            lanes = inverse[j : j + 1, :]
            factor = jnp.sum(
                jnp.where(diagonal, jnp.broadcast_to(lanes, (block, block)), 0.0),
                axis=1,
                keepdims=True,
            )
            at = slice(j * block, (j + 1) * block)
            for h in range(heads):
                value = part_ref[t * heads + h, at].astype(jnp.float32) + sib[0, h, at].astype(
                    jnp.float32
                )
                for d in range(1, chips):
                    value = value + cross_in[d - 1, h, at].astype(jnp.float32)
                kv[h, at] = (value * factor).astype(jnp.bfloat16)

    def load_block(h):
        return lambda p: kv[h, pl.ds(pl.multiple_of(p * block, block), block)]

    def serve(d, carry):
        query_copy(d).wait_recv()
        aux_copy(d).wait_recv()
        for h in range(heads):
            top, total = attend(
                query_in[d - 1, h],
                load_block(h),
                lambda p: (
                    aux_in[d - 1, pl.ds(p, 1), :],
                    aux_in[d - 1, pl.ds(blocks_dev + p, 1), :],
                ),
                aux_in[d - 1, 2 * blocks_dev : 2 * blocks_dev + 1, :],
                blocks_dev,
            )
            back_out[d - 1, h] = acc[...].astype(jnp.bfloat16)
            stat_out[d - 1, h] = jnp.concatenate(
                [top, total, jnp.zeros((6, cols), jnp.float32)], axis=0
            )
        back_copy(d).start()
        stat_copy(d).start()
        return carry

    lax.fori_loop(1, sections, serve, 0)
    own_stats = []
    for h in range(heads):
        stat = attend(
            query_ref[h],
            load_block(h),
            lambda p: (
                aux_ref[me, pl.ds(p, 1), :],
                aux_ref[me, pl.ds(blocks_dev + p, 1), :],
            ),
            rest_own,
            blocks_dev,
        )
        own_stats.append(stat)
        own_acc[h] = acc[...]

    for d in range(1, sections):
        back_copy(d).wait_recv()
        stat_copy(d).wait_recv()
    for h in range(heads):
        tops = [res_stats[h][0], own_stats[h][0]]
        totals = [res_stats[h][1], own_stats[h][1]]
        for d in range(1, sections):
            tops.append(stat_in[d - 1, h, 0:1, :])
            totals.append(stat_in[d - 1, h, 1:2, :])
        top = functools.reduce(jnp.maximum, tops)
        factors = [jnp.exp(one - top) for one in tops]
        total = sum(f * one for f, one in zip(factors, totals))
        mixed = res_acc[h] * factors[0] + own_acc[h] * factors[1]
        for d in range(1, sections):
            mixed = mixed + back_in[d - 1, h].astype(jnp.float32) * factors[d + 1]
        out_ref[h] = jnp.transpose(mixed / total)

    for d in range(chips):
        for i in range(chunks):
            sib_copy(d, i).wait_send()
            if d:
                cross_copy(d, i).wait_send()
    for d in range(1, tp):
        sq_copy(d).wait_send()
    for d in range(1, sections):
        query_copy(d).wait_send()
        aux_copy(d).wait_send()
        back_copy(d).wait_send()
        stat_copy(d).wait_send()


def per_device(
    sections,
    tp,
    tokens,
    norm_gain,
    kv_weight,
    block_owner,
    resident_cache,
    page_table,
    context_len,
    decode_query,
    new_kv,
):
    heads, pool, block, lanes = resident_cache.shape
    _, requests, group_size, dim = decode_query.shape
    cols = requests * group_size
    rows = tokens.shape[0]
    blocks_dev = rows // block
    chunk = min(rows, 256)
    chunks = rows // chunk
    chips = tp // 2
    widened = tokens.astype(jnp.float32)
    squares = jnp.sum(widened * widened, axis=1).reshape(blocks_dev, block)
    normed = (widened * norm_gain.astype(jnp.float32)[None, :]).astype(jnp.bfloat16)
    part = jnp.einsum(
        "td,dhc->htc", normed, kv_weight, preferred_element_type=jnp.float32
    ).astype(jnp.bfloat16)
    full, edge, misc = page_counts(
        page_table, context_len, block_owner[:, 0], sections, pool, block, group_size
    )
    aux = jnp.concatenate(
        [
            full[pool:].reshape(sections, blocks_dev, cols),
            edge[pool:].reshape(sections, blocks_dev, cols),
            jnp.broadcast_to(misc[None], (sections, 8, cols)),
        ],
        axis=1,
    )
    aux_rows = aux.shape[1]
    vmem = pl.BlockSpec(memory_space=pltpu.VMEM)
    dma = pltpu.SemaphoreType.DMA
    peers = sections - 1
    bf16, f32 = jnp.bfloat16, jnp.float32
    out = pl.pallas_call(
        functools.partial(kernel, sections, tp, heads, block, chunk),
        out_shape=jax.ShapeDtypeStruct((heads, cols, dim), f32),
        in_specs=[vmem, vmem, vmem, pl.BlockSpec(memory_space=pl.ANY), vmem, vmem, vmem, vmem],
        out_specs=vmem,
        scratch_shapes=[
            pltpu.VMEM((chips, heads, rows, lanes), bf16),
            pltpu.VMEM((chips - 1, heads, rows, lanes), bf16),
            pltpu.VMEM((chips - 1, heads, rows, lanes), bf16),
            pltpu.VMEM((tp - 1, blocks_dev, block), f32),
            pltpu.VMEM((peers, heads, cols, dim), bf16),
            pltpu.VMEM((peers, aux_rows, cols), f32),
            pltpu.VMEM((heads, rows, lanes), bf16),
            pltpu.VMEM((heads, pool, block, lanes), bf16),
            pltpu.VMEM((max(pool, blocks_dev) * block, cols), f32),
            pltpu.VMEM((dim, cols), f32),
            pltpu.VMEM((heads, dim, cols), f32),
            pltpu.VMEM((peers, heads, dim, cols), bf16),
            pltpu.VMEM((peers, heads, dim, cols), bf16),
            pltpu.VMEM((peers, heads, 8, cols), f32),
            pltpu.VMEM((peers, heads, 8, cols), f32),
            pltpu.VMEM((heads, dim, cols), f32),
            dma((chips, chunks)), dma((chips, chunks)),
            dma((chips - 1, chunks)), dma((chips - 1, chunks)),
            dma((tp - 1,)), dma((tp - 1,)),
            dma((peers,)), dma((peers,)),
            dma((peers,)), dma((peers,)),
            dma((peers,)), dma((peers,)),
            dma((peers,)), dma((peers,)),
            dma(()),
        ],
        compiler_params=pltpu.CompilerParams(
            collective_id=0, has_side_effects=True, vmem_limit_bytes=48 * 1024 * 1024
        ),
    )(
        part,
        squares,
        decode_query.reshape(heads, cols, dim),
        resident_cache,
        new_kv,
        full[:pool],
        edge[:pool],
        aux,
    )
    return out.reshape(heads, requests, group_size, dim)


def solution(mesh):
    sizes = dict(mesh.shape)
    return jax.shard_map(
        functools.partial(per_device, sizes["section"], sizes["tp"]),
        mesh=mesh,
        in_specs=(
            P(("groups", "section"), "tp"),
            P("tp"),
            P("tp", None, None),
            P("groups", None),
            P("tp", ("groups", "section"), None, None),
            P(("groups", "section"), None),
            P(("groups", "section")),
            P("tp", ("groups", "section"), None, None),
            P("tp", ("groups", "section"), None),
        ),
        out_specs=P("tp", ("groups", "section"), None, None),
        check_vma=False,
    )
```

time: 223 us -> 71.5 us (0.32)
  waiting for transfers between devices: 114 us -> 0 us
  Pallas kernels: 0 us -> 48.5 us
  local copies, waits for them, and re-layouts: 42.8 us -> 3.29 us
  matrix products: 33.2 us -> 12.6 us
  between operations: 13.6 us -> 0.12 us
  blocking collectives: 8.35 us -> 0 us
  other arithmetic: 10.4 us -> 6.68 us
    all_gather x1 -> x0, waiting for transfers between devices: 78.6 us -> none  [per_device(): shard_rows = lax.all_gather(blocks, 'section', axis=1, tiled=True)]
    pallas_call x0 -> x1, Pallas kernels: none -> 48.5 us  [per_device(): pl.pallas_call(functools.partial(kernel, sections, tp, heads, block, chun...]
    gather x2 -> x0, local copies, waits for them, and re-layouts: 39.6 us -> none  [attend(): page_pool[:, table].reshape(heads_dev, requests, length, 2 * head_dim)]
    reduce_scatter x1 -> x0, waiting for transfers between devices: 35.8 us -> none  [per_device(): lax.psum_scatter(jnp.einsum('td,dhc->htc', normed, kv_weight, preferred_e...]
    dot_general x4 -> x0, matrix products: 19.3 us -> none  [the longest x1 8.13 us: attend(): jnp.einsum('hrgd,hrld->hrgl', queries, cache_keys, preferred_element_type...]
    psum x1 -> x0, blocking collectives: 8.35 us -> none  [per_device(): squares = lax.psum(local_squares, 'tp')]
    concatenate x1 -> x3, other arithmetic: 3.13 us -> 0.16 us  [the longest x1 0.08 us: page_counts(): pages = jnp.concatenate([jnp.arange(pool, dtype=jnp.int32), placed])]
  transfers between devices with their start and end apart: 2 -> 0, of which waited for: 2 -> 0; matrix products, arithmetic and copies ran while one was open for 2% -> 0% of each run, Pallas kernels for 0% -> 0%
where the time goes in v1:
time: 71.5 us; the launch traced here: 71.2 us
  Pallas kernels  48.5 us (68%)
  matrix products  12.6 us (18%)
  other arithmetic  6.68 us (9%)
  local copies, waits for them, and re-layouts  3.29 us (5%)
    pallas_call x1, Pallas kernels, per_device(): pl.pallas_call(functools.partial(kernel, sections, tp, heads, block, chun...  48.5 us
    dot_general x1, matrix products, per_device(): jnp.einsum('td,dhc->htc', normed, kv_weight, preferred_element_type=jnp.f...  12.6 us
    reduce_sum x1, other arithmetic, per_device(): squares = jnp.sum(widened * widened, axis=1).reshape(blocks_dev, block)  3.07 us

profile of v1, /device:TPU:0, one launch (start us, length us, event | category | flops | bytes accessed | tf_op | source)
XLA Modules:
  0.0 71.2 jit_solution(5718423021152533777)
XLA Ops:
  0.0 0.5 broadcast.150
  0.5 1.3 %reduce.3 = s32[32]{0:T(128)S(1)} reduce(s32[32,1]{0,1:T(1,128)} %param.12, s32[]{:T(128)} %broadcast.150), dimensions={1}, to_apply=%param.12.reduce_sub_computation.3 | reduce | bytes 260 | tf_op args[3]
  1.8 0.1 pad.5.clone
  1.9 0.1 eq.44
  2.0 0.2 convert_reduce_fusion.2
  2.2 0.1 reshape.226
  2.3 0.7 bitcast_select_fusion
  3.0 0.1 pad_add_fusion
  3.1 3.1 %fusion.1 = f32[1024]{0:T(1024)S(1)} fusion(bf16[1024,2048]{1,0:T(8,128)(2,1)} %param.9), kind=kLoop, calls=%fused_computation.3 | loop fusion | flops 6290432 | bytes 4198400 | tf_op jit(solution)/shard_map/reduce_sum | solution.py:394
  6.1 0.7 convert_element_type.49
  6.8 0.7 %broadcast_in_dim.11 = s32[32,8]{1,0:T(8,128)S(1)} broadcast(s32[32]{0:T(128)} %param.15), dimensions={0} | broadcast | bytes 1152 | tf_op jit(solution)/shard_map/broadcast_in_dim | solution.py:38
  7.5 0.1 broadcast_in_dim_reshape.4
  7.6 0.1 le.23
  7.8 0.1 broadcast_compare_fusion
  7.8 0.8 %broadcast_in_dim.10 = s32[8,32,8]{2,1,0:T(8,128)S(1)} broadcast(s32[8,32]{1,0:T(8,128)} %bitcast.23), dimensions={0,1} | broadcast | bytes 9216 | tf_op jit(solution)/shard_map/broadcast_in_dim | solution.py:37
  8.6 0.1 eq.49
  8.7 0.4 convert_reduce_fusion
  9.2 0.1 maximum_maximum_fusion
  9.3 0.0 copy-start
  9.3 0.0 copy-start.1
  9.3 12.6 %convert_bitcast_fusion.part_ref = bf16[8,1024,256]{2,1,0:T(8,128)(2,1)S(1)} fusion(bf16[2048,8,256]{2,1,0:T(8,128)(2,1)} %param.11, bf16[1024,2048]{1,0:T(8,128)(2,1)} %param.9, f32[2048]{0:T(1024)S(1)} %convert_element_type.49), kind=kOutput, calls=%fused_computation.7 | convolution fusion | flops 8598323200 | bytes 16785408 | tf_op jit(solution)/shard_map/td,dhc->htc/dot_general | solution.py:396
  22.0 0.0 copy-done
  22.0 0.0 copy-done.1
  22.0 48.5 %shard_map.91 = f32[2,256,128]{2,1,0:T(8,128)S(1)} custom-call(bf16[8,1024,256]{2,1,0:T(8,128)(2,1)S(1)} %convert_bitcast_fusion.part_ref, f32[8,128]{1,0:T(8,128)S(1)} %bitcast.21, bf16[2,256,128]{2,1,0:T(8,128)(2,1)S(1)} %bitcast.20, bf16[2,32,128,256]{3,2,1,0:T(8,128)(2,1)} %cache_ref.1, bf16[2,32,256]{2,1,0:T(8,128)(2,1)S(1)} %copy-done.1, ...), custom_call_target="tpu_custom_call" | custom-call | tf_op jit(solution)/shard_map/pallas_call | solution.py:415
  70.5 0.7 copy.18
  (12 shorter events, 0.1 us)
Async XLA Ops:
  9.3 12.7 %copy-start = (bf16[2,32,8,128]{3,2,1,0:T(8,128)(2,1)S(1)}, bf16[2,32,8,128]{3,2,1,0:T(8,128)(2,1)}, u32[]{:S(2)}) copy-start(bf16[2,32,8,128]{3,2,1,0:T(8,128)(2,1)} %param.16) | copy-start | bytes 393220
  9.3 12.7 %copy-start.1 = (bf16[2,32,256]{2,1,0:T(8,128)(2,1)S(1)}, bf16[2,32,256]{2,1,0:T(8,128)(2,1)}, u32[]{:S(2)}) copy-start(bf16[2,32,256]{2,1,0:T(8,128)(2,1)} %fresh_ref.1) | copy-start | bytes 98308

commit v2 on v1

--- a/solution.py
+++ b/solution.py
@@ -17,45 +17,75 @@
 MESH = pl.DeviceIdType.MESH
 
 
-def block_ranks(owner_grid):
-    blocks_dev = owner_grid.shape[1]
-    same_owner = owner_grid[:, :, None] == owner_grid[:, None, :]
-    positions = jnp.arange(blocks_dev, dtype=jnp.int32)
-    earlier = positions[None, :] < positions[:, None]
-    return jnp.sum((same_owner & earlier[None]).astype(jnp.int32), axis=2)
-
-
-def page_counts(table, lengths, owner_flat, sections, pool, block, group_size):
-    blocks_dev = owner_flat.shape[0] // sections
+def count_pages(
+    sections, heads, pool, block, owner_ref, table_ref, length_ref, full_ref, edge_ref, aux_ref
+):
+    total_blocks = owner_ref.shape[0]
+    blocks_dev = total_blocks // sections
     slots_peer = 2 * ((blocks_dev + sections - 1) // sections)
-    rank = block_ranks(owner_flat.reshape(sections, blocks_dev)).reshape(-1)
-    ids = jnp.arange(owner_flat.shape[0], dtype=jnp.int32)
-    placed = jnp.where(
-        owner_flat == lax.axis_index("section"), pool + ids // blocks_dev * slots_peer + rank, -1
+    requests, depth = table_ref.shape
+    cols = full_ref.shape[1]
+    me = lax.axis_index("section")
+    f32 = jnp.float32
+
+    def iota(shape, axis):
+        return lax.broadcasted_iota(jnp.int32, shape, axis)
+
+    grid = (total_blocks, total_blocks)
+    across = jnp.broadcast_to(owner_ref[...], grid)
+    row, column = iota(grid, 0), iota(grid, 1)
+    along = jnp.sum(jnp.where(row == column, across, 0).astype(f32), axis=0, keepdims=True)
+    earlier = (across.astype(f32) == along) & (column < row)
+    earlier = earlier & (lax.div(column, blocks_dev) == lax.div(row, blocks_dev))
+    rank = jnp.sum(jnp.where(earlier, 1.0, 0.0), axis=1, keepdims=True)
+    tall = (total_blocks, 1)
+    slot = pool + lax.div(iota(tall, 0), blocks_dev) * slots_peer
+    placed = jnp.where(owner_ref[...] == me, slot.astype(f32) + rank, -1.0)
+
+    spread = iota((requests, cols), 0) == lax.div(iota((requests, cols), 1), cols // requests)
+    spread = jnp.where(spread, 1.0, 0.0)
+    contract = (((0,), (0,)), ((), ()))
+    columns = lax.dot_general(
+        table_ref[...].astype(f32), spread, contract, preferred_element_type=f32
     )
-    pages = jnp.concatenate([jnp.arange(pool, dtype=jnp.int32), placed])
-    columns = jnp.repeat(table.T, group_size, axis=1)
-    length = jnp.repeat(lengths, group_size)[None]
-    begin = jnp.arange(columns.shape[0], dtype=jnp.int32)[:, None] * block
-    whole = begin + block <= length
-    partial = (begin < length) & ~whole
-    same = pages[:, None, None] == columns[None]
-    full = jnp.sum((same & whole[None]).astype(jnp.float32), axis=1)
-    edge = jnp.sum((same & partial[None]).astype(jnp.float32), axis=1)
-    rest = (length % block).astype(jnp.float32)
-    zeros = length.astype(jnp.float32) - jnp.sum(full * block + edge * rest, axis=0, keepdims=True)
-    misc = jnp.concatenate([rest, zeros, jnp.zeros((6, rest.shape[1]), jnp.float32)], axis=0)
-    return full, edge, misc
+    length = jnp.broadcast_to(length_ref[...], (8, requests))
+    split = lax.div(length, block)
+    blocks_held = jnp.dot(split.astype(f32), spread, preferred_element_type=f32)[:1]
+    rest = jnp.dot((length - split * block).astype(f32), spread, preferred_element_type=f32)[:1]
+
+    def counts(pages):
+        full = jnp.zeros((pages.shape[0], cols), f32)
+        edge = jnp.zeros((pages.shape[0], cols), f32)
+        for j in range(depth):
+            same = jnp.where(pages == columns[j : j + 1], 1.0, 0.0)
+            full = full + jnp.where(blocks_held > j, same, 0.0)
+            edge = edge + jnp.where(blocks_held == j, same, 0.0)
+        return full, edge
+
+    full, edge = counts(iota((pool, 1), 0).astype(f32))
+    full_ref[...] = full
+    edge_ref[...] = edge
+    zeros = (blocks_held * block + rest) - jnp.sum(full * block + edge * rest, axis=0, keepdims=True)
+    full, edge = counts(placed)
+    zeros = zeros - jnp.sum(full * block + edge * rest, axis=0, keepdims=True)
+    for s in range(sections):
+        at = slice(s * blocks_dev, (s + 1) * blocks_dev)
+        aux_ref[s, :blocks_dev] = full[at]
+        aux_ref[s, blocks_dev : 2 * blocks_dev] = edge[at]
+        aux_ref[s, 2 * blocks_dev :] = jnp.concatenate(
+            [rest, zeros, jnp.zeros((6, cols), f32)], axis=0
+        )
 
 
 def kernel(
     sections, tp, heads, block, chunk,
-    part_ref, sq_ref, query_ref, cache_ref, fresh_ref, full_ref, edge_ref, aux_ref,
+    part_ref, token_ref, query_ref, cache_ref, fresh_ref, owner_ref, table_ref, length_ref,
     out_ref,
+    tokens, sq_ref, full_ref, edge_ref, aux_ref,
     sib, cross_out, cross_in, sq_in, query_in, aux_in, kv, pages, scores, acc, res_acc,
     back_out, back_in, stat_out, stat_in, own_acc,
     sib_s, sib_r, cross_s, cross_r, sq_s, sq_r, query_s, query_r, aux_s, aux_r,
-    back_s, back_r, stat_s, stat_r, page_s,
+    back_s, back_r, stat_s, stat_r, page_s, token_s,
 ):
     me = lax.axis_index("section")
     t = lax.axis_index("tp")
@@ -83,23 +113,23 @@
     def span(i):
         return pl.ds(pl.multiple_of(i * chunk, chunk), chunk)
 
-    def sib_copy(d, i):
+    def sib_copy(d, h, i):
         group = lax.rem(x + d, chips) * 2 + 1 - core
         return pltpu.make_async_remote_copy(
-            src_ref=part_ref.at[pl.ds(group * heads, heads), span(i)],
-            dst_ref=sib.at[d, :, span(i)],
-            send_sem=sib_s.at[d, i],
-            recv_sem=sib_r.at[d, i],
+            src_ref=part_ref.at[group * heads + h, span(i)],
+            dst_ref=sib.at[d, h, span(i)],
+            send_sem=sib_s.at[d, h, i],
+            recv_sem=sib_r.at[d, h, i],
             device_id={"tp": x * 2 + 1 - core},
             device_id_type=MESH,
         )
 
-    def cross_copy(d, i):
-        return pltpu.make_async_remote_copy(
-            src_ref=cross_out.at[d - 1, :, span(i)],
-            dst_ref=cross_in.at[d - 1, :, span(i)],
-            send_sem=cross_s.at[d - 1, i],
-            recv_sem=cross_r.at[d - 1, i],
+    def cross_copy(d, h, i):
+        return pltpu.make_async_remote_copy(
+            src_ref=cross_out.at[d - 1, h, span(i)],
+            dst_ref=cross_in.at[d - 1, h, span(i)],
+            send_sem=cross_s.at[d - 1, h, i],
+            recv_sem=cross_r.at[d - 1, h, i],
             device_id={"tp": lax.rem(x + d, chips) * 2 + core},
             device_id_type=MESH,
         )
@@ -135,22 +165,22 @@
             device_id_type=MESH,
         )
 
-    def back_copy(d):
-        return pltpu.make_async_remote_copy(
-            src_ref=back_out.at[d - 1],
-            dst_ref=back_in.at[d - 1],
-            send_sem=back_s.at[d - 1],
-            recv_sem=back_r.at[d - 1],
+    def back_copy(d, h):
+        return pltpu.make_async_remote_copy(
+            src_ref=back_out.at[d - 1, h],
+            dst_ref=back_in.at[d - 1, h],
+            send_sem=back_s.at[d - 1, h],
+            recv_sem=back_r.at[d - 1, h],
             device_id={"section": lax.rem(me + sections - d, sections)},
             device_id_type=MESH,
         )
 
-    def stat_copy(d):
-        return pltpu.make_async_remote_copy(
-            src_ref=stat_out.at[d - 1],
-            dst_ref=stat_in.at[d - 1],
-            send_sem=stat_s.at[d - 1],
-            recv_sem=stat_r.at[d - 1],
+    def stat_copy(d, h):
+        return pltpu.make_async_remote_copy(
+            src_ref=stat_out.at[d - 1, h],
+            dst_ref=stat_in.at[d - 1, h],
+            send_sem=stat_s.at[d - 1, h],
+            recv_sem=stat_r.at[d - 1, h],
             device_id={"section": lax.rem(me + sections - d, sections)},
             device_id_type=MESH,
         )
@@ -158,28 +188,57 @@
     def page_copy():
         return pltpu.make_async_copy(cache_ref, pages, page_s)
 
-    for d in range(1, chips):
+    def token_copy():
+        return pltpu.make_async_copy(token_ref, tokens, token_s)
+
+    for h in range(heads):
+        for d in range(1, chips):
+            for i in range(chunks):
+                sib_copy(d, h, i).start()
+    token_copy().start()
+    page_copy().start()
+    for d in range(1, sections):
+        query_copy(d).start()
+
+    count_pages(
+        sections, heads, pool, block, owner_ref, table_ref, length_ref, full_ref, edge_ref, aux_ref
+    )
+    for d in range(1, sections):
+        aux_copy(d).start()
+
+    def cross(h):
+        for d in range(1, chips):
+            group = lax.rem(x + d, chips) * 2 + core
+            for i in range(chunks):
+                sib_copy(d, h, i).wait_recv()
+                mine = part_ref[group * heads + h, span(i)]
+                theirs = sib[d, h, span(i)]
+                cross_out[d - 1, h, span(i)] = (
+                    mine.astype(jnp.float32) + theirs.astype(jnp.float32)
+                ).astype(jnp.bfloat16)
+                if h == 0:
+                    cross_copy(d, h, i).start()
+
+    for h in range(heads):
+        cross(h)
+    for h in range(heads):
         for i in range(chunks):
-            sib_copy(d, i).start()
+            sib_copy(0, h, i).start()
+
+    token_copy().wait()
+
+    def square(j, carry):
+        total = jnp.zeros((block, 128), jnp.float32)
+        at = pl.ds(pl.multiple_of(j * block, block), block)
+        for k in range(tokens.shape[1] // 128):
+            piece = tokens[at, k * 128 : (k + 1) * 128].astype(jnp.float32)
+            total = total + piece * piece
+        sq_ref[pl.ds(j, 1), :] = jnp.sum(jnp.transpose(total), axis=0, keepdims=True)
+        return carry
+
+    lax.fori_loop(0, blocks_dev, square, 0)
     for d in range(1, tp):
         sq_copy(d).start()
-    page_copy().start()
-    for i in range(chunks):
-        sib_copy(0, i).start()
-    for d in range(1, sections):
-        query_copy(d).start()
-        aux_copy(d).start()
-
-    for d in range(1, chips):
-        group = lax.rem(x + d, chips) * 2 + core
-        for i in range(chunks):
-            sib_copy(d, i).wait_recv()
-            mine = part_ref[pl.ds(group * heads, heads), span(i)]
-            theirs = sib[d, :, span(i)]
-            cross_out[d - 1, :, span(i)] = (
-                mine.astype(jnp.float32) + theirs.astype(jnp.float32)
-            ).astype(jnp.bfloat16)
-            cross_copy(d, i).start()
 
     position = lax.broadcasted_iota(jnp.int32, (block, cols), 0).astype(jnp.float32)
 
@@ -276,20 +335,31 @@
         jnp.int32, (block, block), 1
     )
     per_chunk = chunk // block
-    for i in range(chunks):
-        sib_copy(0, i).wait_recv()
-        for d in range(1, chips):
-            cross_copy(d, i).wait_recv()
-        for k in range(per_chunk):
-            j = i * per_chunk + k
-            lanes = inverse[j : j + 1, :]
-            factor = jnp.sum(
-                jnp.where(diagonal, jnp.broadcast_to(lanes, (block, block)), 0.0),
-                axis=1,
-                keepdims=True,
-            )
-            at = slice(j * block, (j + 1) * block)
-            for h in range(heads):
+
+    def load_block(h):
+        return lambda p: kv[h, pl.ds(pl.multiple_of(p * block, block), block)]
+
+    for h in range(heads):
+        if h + 1 < heads:
+            for d in range(1, chips):
+                for i in range(chunks):
+                    cross_copy(d, h, i).wait_send()
+            for d in range(1, chips):
+                for i in range(chunks):
+                    cross_copy(d, h + 1, i).start()
+        for i in range(chunks):
+            sib_copy(0, h, i).wait_recv()
+            for d in range(1, chips):
+                cross_copy(d, h, i).wait_recv()
+            for k in range(per_chunk):
+                j = i * per_chunk + k
+                lanes = inverse[j : j + 1, :]
+                factor = jnp.sum(
+                    jnp.where(diagonal, jnp.broadcast_to(lanes, (block, block)), 0.0),
+                    axis=1,
+                    keepdims=True,
+                )
+                at = slice(j * block, (j + 1) * block)
                 value = part_ref[t * heads + h, at].astype(jnp.float32) + sib[0, h, at].astype(
                     jnp.float32
                 )
@@ -297,13 +367,10 @@
                     value = value + cross_in[d - 1, h, at].astype(jnp.float32)
                 kv[h, at] = (value * factor).astype(jnp.bfloat16)
 
-    def load_block(h):
-        return lambda p: kv[h, pl.ds(pl.multiple_of(p * block, block), block)]
-
-    def serve(d, carry):
-        query_copy(d).wait_recv()
-        aux_copy(d).wait_recv()
-        for h in range(heads):
+        def serve(d, carry, h=h):
+            if h == 0:
+                query_copy(d).wait_recv()
+                aux_copy(d).wait_recv()
             top, total = attend(
                 query_in[d - 1, h],
                 load_block(h),
@@ -318,11 +385,12 @@
             stat_out[d - 1, h] = jnp.concatenate(
                 [top, total, jnp.zeros((6, cols), jnp.float32)], axis=0
             )
-        back_copy(d).start()
-        stat_copy(d).start()
-        return carry
-
-    lax.fori_loop(1, sections, serve, 0)
+            back_copy(d, h).start()
+            stat_copy(d, h).start()
+            return carry
+
+        lax.fori_loop(1, sections, serve, 0)
+
     own_stats = []
     for h in range(heads):
         stat = attend(
@@ -338,10 +406,10 @@
         own_stats.append(stat)
         own_acc[h] = acc[...]
 
-    for d in range(1, sections):
-        back_copy(d).wait_recv()
-        stat_copy(d).wait_recv()
-    for h in range(heads):
+    for h in range(heads):
+        for d in range(1, sections):
+            back_copy(d, h).wait_recv()
+            stat_copy(d, h).wait_recv()
         tops = [res_stats[h][0], own_stats[h][0]]
         totals = [res_stats[h][1], own_stats[h][1]]
         for d in range(1, sections):
@@ -355,18 +423,20 @@
             mixed = mixed + back_in[d - 1, h].astype(jnp.float32) * factors[d + 1]
         out_ref[h] = jnp.transpose(mixed / total)
 
-    for d in range(chips):
+    for h in range(heads):
         for i in range(chunks):
-            sib_copy(d, i).wait_send()
-            if d:
-                cross_copy(d, i).wait_send()
+            for d in range(chips):
+                sib_copy(d, h, i).wait_send()
+                if d and h == heads - 1:
+                    cross_copy(d, h, i).wait_send()
     for d in range(1, tp):
         sq_copy(d).wait_send()
     for d in range(1, sections):
         query_copy(d).wait_send()
         aux_copy(d).wait_send()
-        back_copy(d).wait_send()
-        stat_copy(d).wait_send()
+        for h in range(heads):
+            back_copy(d, h).wait_send()
+            stat_copy(d, h).wait_send()
 
 
 def per_device(
@@ -387,37 +457,31 @@
     cols = requests * group_size
     rows = tokens.shape[0]
     blocks_dev = rows // block
-    chunk = min(rows, 256)
+    chunk = min(rows, 512)
     chunks = rows // chunk
     chips = tp // 2
     widened = tokens.astype(jnp.float32)
-    squares = jnp.sum(widened * widened, axis=1).reshape(blocks_dev, block)
     normed = (widened * norm_gain.astype(jnp.float32)[None, :]).astype(jnp.bfloat16)
     part = jnp.einsum(
         "td,dhc->htc", normed, kv_weight, preferred_element_type=jnp.float32
     ).astype(jnp.bfloat16)
-    full, edge, misc = page_counts(
-        page_table, context_len, block_owner[:, 0], sections, pool, block, group_size
-    )
-    aux = jnp.concatenate(
-        [
-            full[pool:].reshape(sections, blocks_dev, cols),
-            edge[pool:].reshape(sections, blocks_dev, cols),
-            jnp.broadcast_to(misc[None], (sections, 8, cols)),
-        ],
-        axis=1,
-    )
-    aux_rows = aux.shape[1]
+    aux_rows = 2 * blocks_dev + 8
     vmem = pl.BlockSpec(memory_space=pltpu.VMEM)
+    anywhere = pl.BlockSpec(memory_space=pl.ANY)
     dma = pltpu.SemaphoreType.DMA
     peers = sections - 1
     bf16, f32 = jnp.bfloat16, jnp.float32
     out = pl.pallas_call(
         functools.partial(kernel, sections, tp, heads, block, chunk),
         out_shape=jax.ShapeDtypeStruct((heads, cols, dim), f32),
-        in_specs=[vmem, vmem, vmem, pl.BlockSpec(memory_space=pl.ANY), vmem, vmem, vmem, vmem],
+        in_specs=[vmem, anywhere, vmem, anywhere, vmem, vmem, vmem, vmem],
         out_specs=vmem,
         scratch_shapes=[
+            pltpu.VMEM(tokens.shape, bf16),
+            pltpu.VMEM((blocks_dev, block), f32),
+            pltpu.VMEM((pool, cols), f32),
+            pltpu.VMEM((pool, cols), f32),
+            pltpu.VMEM((sections, aux_rows, cols), f32),
             pltpu.VMEM((chips, heads, rows, lanes), bf16),
             pltpu.VMEM((chips - 1, heads, rows, lanes), bf16),
             pltpu.VMEM((chips - 1, heads, rows, lanes), bf16),
@@ -434,13 +498,14 @@
             pltpu.VMEM((peers, heads, 8, cols), f32),
             pltpu.VMEM((peers, heads, 8, cols), f32),
             pltpu.VMEM((heads, dim, cols), f32),
-            dma((chips, chunks)), dma((chips, chunks)),
-            dma((chips - 1, chunks)), dma((chips - 1, chunks)),
+            dma((chips, heads, chunks)), dma((chips, heads, chunks)),
+            dma((chips - 1, heads, chunks)), dma((chips - 1, heads, chunks)),
             dma((tp - 1,)), dma((tp - 1,)),
             dma((peers,)), dma((peers,)),
             dma((peers,)), dma((peers,)),
-            dma((peers,)), dma((peers,)),
-            dma((peers,)), dma((peers,)),
+            dma((peers, heads)), dma((peers, heads)),
+            dma((peers, heads)), dma((peers, heads)),
+            dma(()),
             dma(()),
         ],
         compiler_params=pltpu.CompilerParams(
@@ -448,13 +513,13 @@
         ),
     )(
         part,
-        squares,
+        tokens,
         decode_query.reshape(heads, cols, dim),
         resident_cache,
         new_kv,
-        full[:pool],
-        edge[:pool],
-        aux,
+        block_owner,
+        page_table,
+        context_len.reshape(1, requests),
     )
     return out.reshape(heads, requests, group_size, dim)
 

time: 71.5 us -> 59 us (0.83)
  other arithmetic: 6.68 us -> 0.69 us
  Pallas kernels: 48.5 us -> 43.2 us
  local copies, waits for them, and re-layouts: 3.29 us -> 2.21 us
    pallas_call x1, Pallas kernels: 48.5 us -> 43.2 us  [per_device(): pl.pallas_call(functools.partial(kernel, sections, tp, heads, block, chun...]
    reduce_sum x4 -> x0, other arithmetic: 3.73 us -> none  [the longest x1 3.07 us: per_device(): squares = jnp.sum(widened * widened, axis=1).reshape(blocks_dev, block)]
    broadcast_in_dim x4 -> x0, local copies, waits for them, and re-layouts: 1.51 us -> none  [the longest x1 0.77 us: page_counts(): columns = jnp.repeat(table.T, group_size, axis=1)]
    unnamed x1 -> x0, other arithmetic: 1.32 us -> none
    unnamed x6 -> x9, local copies, waits for them, and re-layouts: 1.23 us -> 2.21 us
where the time goes in v2:
time: 59 us; the launch traced here: 58.7 us
  Pallas kernels  43.2 us (73%)
  matrix products  12.6 us (21%)
  local copies, waits for them, and re-layouts  2.21 us (4%)
  other arithmetic  0.69 us (1%)
    pallas_call x1, Pallas kernels, per_device(): pl.pallas_call(functools.partial(kernel, sections, tp, heads, block, chun...  43.2 us
    dot_general x1, matrix products, per_device(): jnp.einsum('td,dhc->htc', normed, kv_weight, preferred_element_type=jnp.f...  12.6 us
    unnamed x9, local copies, waits for them, and re-layouts  2.21 us

profile of v2, /device:TPU:0, one launch (start us, length us, event | category | flops | bytes accessed | tf_op | source)
XLA Modules:
  0.0 58.7 jit_solution(3425369444628595524)
XLA Ops:
  0.0 0.7 %convert_element_type.15 = f32[2048]{0:T(1024)S(1)} convert(bf16[2048]{0:T(1024)(128)(2,1)} %param.10) | non-fusion elementwise | flops 2048 | bytes 12288 | tf_op jit(solution)/shard_map/convert_element_type | solution.py:464
  0.7 0.7 %copy.11.owner_ref = s32[32,1]{1,0:T(8,128)S(1)} copy(s32[32,1]{0,1:T(1,128)} %param.12) | data formatting | bytes 256 | tf_op args[3]
  1.4 0.8 %copy.12.table_ref = s32[32,8]{1,0:T(8,128)S(1)} copy(s32[32,8]{0,1:T(8,128)} %param.14) | data formatting | bytes 2048 | tf_op args[5]
  2.2 0.0 copy-start
  2.2 0.0 copy-start.1
  2.2 0.0 copy-start.2
  2.2 12.6 %convert_bitcast_fusion.part_ref = bf16[8,1024,256]{2,1,0:T(8,128)(2,1)S(1)} fusion(bf16[2048,8,256]{2,1,0:T(8,128)(2,1)} %param.11, bf16[1024,2048]{1,0:T(8,128)(2,1)} %token_ref.1, f32[2048]{0:T(1024)S(1)} %convert_element_type.15), kind=kOutput, calls=%fused_computation.4 | convolution fusion | flops 8598323200 | bytes 16785408 | tf_op jit(solution)/shard_map/td,dhc->htc/dot_general | solution.py:465
  14.8 0.0 copy-done
  14.8 0.0 copy-done.1
  14.8 0.0 copy-done.2
  14.9 43.2 %shard_map.91 = f32[2,256,128]{2,1,0:T(8,128)S(1)} custom-call(bf16[8,1024,256]{2,1,0:T(8,128)(2,1)S(1)} %convert_bitcast_fusion.part_ref, bf16[1024,2048]{1,0:T(8,128)(2,1)} %token_ref.1, bf16[2,256,128]{2,1,0:T(8,128)(2,1)S(1)} %bitcast.11, bf16[2,32,128,256]{3,2,1,0:T(8,128)(2,1)} %cache_ref.1, bf16[2,32,256]{2,1,0:T(8,128)(2,1)S(1)} %copy-done.1, ...), custom_call_target="tpu_custom_call" | custom-call | tf_op jit(solution)/shard_map/pallas_call | solution.py:474
  58.0 0.7 %copy.18 = f32[2,32,8,128]{3,2,1,0:T(8,128)} copy(f32[2,32,8,128]{3,2,1,0:T(8,128)S(1)} %bitcast.10) | data formatting | bytes 524288
Async XLA Ops:
  2.2 12.6 %copy-start = (bf16[2,32,8,128]{3,2,1,0:T(8,128)(2,1)S(1)}, bf16[2,32,8,128]{3,2,1,0:T(8,128)(2,1)}, u32[]{:S(2)}) copy-start(bf16[2,32,8,128]{3,2,1,0:T(8,128)(2,1)} %param.16) | copy-start | bytes 393220
  2.2 12.6 %copy-start.1 = (bf16[2,32,256]{2,1,0:T(8,128)(2,1)S(1)}, bf16[2,32,256]{2,1,0:T(8,128)(2,1)}, u32[]{:S(2)}) copy-start(bf16[2,32,256]{2,1,0:T(8,128)(2,1)} %fresh_ref.1) | copy-start | bytes 98308
  2.2 12.7 %copy-start.2 = (s32[32]{0:T(128)S(1)}, s32[32]{0:T(128)}, u32[]{:S(2)}) copy-start(s32[32]{0:T(128)} %param.15) | copy-start | bytes 388

commit v3 on v2

--- a/solution.py
+++ b/solution.py
@@ -79,13 +79,13 @@
 
 def kernel(
     sections, tp, heads, block, chunk,
-    part_ref, token_ref, query_ref, cache_ref, fresh_ref, owner_ref, table_ref, length_ref,
+    token_ref, gain_ref, weight_ref, query_ref, cache_ref, fresh_ref, owner_ref, table_ref, length_ref,
     out_ref,
-    tokens, sq_ref, full_ref, edge_ref, aux_ref,
+    tokens, raw, weights, part_ref, sq_ref, full_ref, edge_ref, aux_ref,
     sib, cross_out, cross_in, sq_in, query_in, aux_in, kv, pages, scores, acc, res_acc,
     back_out, back_in, stat_out, stat_in, own_acc,
     sib_s, sib_r, cross_s, cross_r, sq_s, sq_r, query_s, query_r, aux_s, aux_r,
-    back_s, back_r, stat_s, stat_r, page_s, token_s,
+    back_s, back_r, stat_s, stat_r, page_s, token_s, raw_s,
 ):
     me = lax.axis_index("section")
     t = lax.axis_index("tp")
@@ -188,14 +188,19 @@
     def page_copy():
         return pltpu.make_async_copy(cache_ref, pages, page_s)
 
-    def token_copy():
-        return pltpu.make_async_copy(token_ref, tokens, token_s)
-
-    for h in range(heads):
-        for d in range(1, chips):
-            for i in range(chunks):
-                sib_copy(d, h, i).start()
-    token_copy().start()
+    raw_rows = raw.shape[0] // blocks_dev
+
+    def token_copy(j):
+        at = pl.ds(pl.multiple_of(j * block, block), block)
+        return pltpu.make_async_copy(token_ref.at[at], tokens.at[at], token_s.at[j])
+
+    def raw_copy(j):
+        at = pl.ds(pl.multiple_of(j * raw_rows, raw_rows), raw_rows)
+        return pltpu.make_async_copy(weight_ref.at[at], raw.at[at], raw_s.at[j])
+
+    for j in range(blocks_dev):
+        raw_copy(j).start()
+        token_copy(j).start()
     page_copy().start()
     for d in range(1, sections):
         query_copy(d).start()
@@ -205,6 +210,48 @@
     )
     for d in range(1, sections):
         aux_copy(d).start()
+
+    all_heads = weights.shape[0]
+    tile = 256
+    deep = tile // all_heads
+    to, at_row = lax.broadcasted_iota(jnp.int32, (tile, tile), 0), lax.broadcasted_iota(
+        jnp.int32, (tile, tile), 1
+    )
+    order = jnp.where(
+        at_row == lax.rem(to, deep) * all_heads + lax.div(to, deep), 1.0, 0.0
+    ).astype(jnp.bfloat16)
+
+    def prepare(j, carry):
+        raw_copy(j).wait()
+        token_copy(j).wait()
+        total = jnp.zeros((block, 128), jnp.float32)
+        at = pl.ds(pl.multiple_of(j * block, block), block)
+        for k in range(tokens.shape[1] // 128):
+            lanes = slice(k * 128, (k + 1) * 128)
+            piece = tokens[at, lanes].astype(jnp.float32)
+            total = total + piece * piece
+            tokens[at, lanes] = (piece * gain_ref[:, lanes]).astype(jnp.bfloat16)
+        sq_ref[pl.ds(j, 1), :] = jnp.sum(jnp.transpose(total), axis=0, keepdims=True)
+        for k in range(raw_rows // tile):
+            first = pl.multiple_of(j * raw_rows + k * tile, tile)
+            rows_k = jnp.dot(
+                order, raw[pl.ds(first, tile)], preferred_element_type=jnp.float32
+            ).astype(jnp.bfloat16)
+            depth = pl.multiple_of(j * (raw_rows // all_heads) + k * deep, deep)
+            weights[:, pl.ds(depth, deep)] = rows_k.reshape(all_heads, deep, raw.shape[1])
+        return carry
+
+    lax.fori_loop(0, blocks_dev, prepare, 0)
+    for d in range(1, tp):
+        sq_copy(d).start()
+
+    def project(head, send):
+        for i in range(chunks):
+            part_ref[head, span(i)] = jnp.dot(
+                tokens[span(i), :], weights[head], preferred_element_type=jnp.float32
+            ).astype(jnp.bfloat16)
+            if send is not None:
+                sib_copy(send[0], send[1], i).start()
 
     def cross(h):
         for d in range(1, chips):
@@ -220,25 +267,15 @@
                     cross_copy(d, h, i).start()
 
     for h in range(heads):
+        for d in range(1, chips):
+            project((lax.rem(x + d, chips) * 2 + 1 - core) * heads + h, (d, h))
+        for d in range(1, chips):
+            project((lax.rem(x + d, chips) * 2 + core) * heads + h, None)
         cross(h)
     for h in range(heads):
-        for i in range(chunks):
-            sib_copy(0, h, i).start()
-
-    token_copy().wait()
-
-    def square(j, carry):
-        total = jnp.zeros((block, 128), jnp.float32)
-        at = pl.ds(pl.multiple_of(j * block, block), block)
-        for k in range(tokens.shape[1] // 128):
-            piece = tokens[at, k * 128 : (k + 1) * 128].astype(jnp.float32)
-            total = total + piece * piece
-        sq_ref[pl.ds(j, 1), :] = jnp.sum(jnp.transpose(total), axis=0, keepdims=True)
-        return carry
-
-    lax.fori_loop(0, blocks_dev, square, 0)
-    for d in range(1, tp):
-        sq_copy(d).start()
+        project((x * 2 + 1 - core) * heads + h, (0, h))
+    for h in range(heads):
+        project(t * heads + h, None)
 
     position = lax.broadcasted_iota(jnp.int32, (block, cols), 0).astype(jnp.float32)
 
@@ -460,11 +497,7 @@
     chunk = min(rows, 512)
     chunks = rows // chunk
     chips = tp // 2
-    widened = tokens.astype(jnp.float32)
-    normed = (widened * norm_gain.astype(jnp.float32)[None, :]).astype(jnp.bfloat16)
-    part = jnp.einsum(
-        "td,dhc->htc", normed, kv_weight, preferred_element_type=jnp.float32
-    ).astype(jnp.bfloat16)
+    features, all_heads, _ = kv_weight.shape
     aux_rows = 2 * blocks_dev + 8
     vmem = pl.BlockSpec(memory_space=pltpu.VMEM)
     anywhere = pl.BlockSpec(memory_space=pl.ANY)
@@ -474,10 +507,13 @@
     out = pl.pallas_call(
         functools.partial(kernel, sections, tp, heads, block, chunk),
         out_shape=jax.ShapeDtypeStruct((heads, cols, dim), f32),
-        in_specs=[vmem, anywhere, vmem, anywhere, vmem, vmem, vmem, vmem],
+        in_specs=[anywhere, vmem, anywhere, vmem, anywhere, vmem, vmem, vmem, vmem],
         out_specs=vmem,
         scratch_shapes=[
             pltpu.VMEM(tokens.shape, bf16),
+            pltpu.VMEM((features * all_heads, lanes), bf16),
+            pltpu.VMEM((all_heads, features, lanes), bf16),
+            pltpu.VMEM((all_heads, rows, lanes), bf16),
             pltpu.VMEM((blocks_dev, block), f32),
             pltpu.VMEM((pool, cols), f32),
             pltpu.VMEM((pool, cols), f32),
@@ -506,14 +542,15 @@
             dma((peers, heads)), dma((peers, heads)),
             dma((peers, heads)), dma((peers, heads)),
             dma(()),
-            dma(()),
+            dma((blocks_dev,)), dma((blocks_dev,)),
         ],
         compiler_params=pltpu.CompilerParams(
-            collective_id=0, has_side_effects=True, vmem_limit_bytes=48 * 1024 * 1024
+            collective_id=0, has_side_effects=True, vmem_limit_bytes=56 * 1024 * 1024
         ),
     )(
-        part,
         tokens,
+        norm_gain.astype(f32).reshape(1, features),
+        kv_weight.reshape(features * all_heads, lanes),
         decode_query.reshape(heads, cols, dim),
         resident_cache,
         new_kv,

time: 59 us -> 67.3 us (1.14)
  Pallas kernels: 43.2 us -> 61.4 us
  matrix products: 12.6 us -> 0 us
  local copies, waits for them, and re-layouts: 2.21 us -> 4.37 us
    pallas_call x1, Pallas kernels: 43.2 us -> 61.4 us  [per_device(): pl.pallas_call(functools.partial(kernel, sections, tp, heads, block, chun...]
    dot_general x1 -> x0, matrix products: 12.6 us -> none  [per_device(): jnp.einsum('td,dhc->htc', normed, kv_weight, preferred_element_type=jnp.f...]
    unnamed x9 -> x3, local copies, waits for them, and re-layouts: 2.21 us -> 4.37 us
    reshape x0 -> x1, other arithmetic: none -> 1.28 us  [per_device(): norm_gain.astype(f32).reshape(1, features)]
    convert_element_type x1 -> x0, other arithmetic: 0.69 us -> none  [per_device(): norm_gain.astype(jnp.float32)[None, :]]
where the time goes in v3:
time: 67.3 us; the launch traced here: 67.1 us
  Pallas kernels  61.4 us (91%)
  local copies, waits for them, and re-layouts  4.37 us (6%)
  other arithmetic  1.28 us (2%)
    pallas_call x1, Pallas kernels, per_device(): pl.pallas_call(functools.partial(kernel, sections, tp, heads, block, chun...  61.4 us
    unnamed x3, local copies, waits for them, and re-layouts  4.37 us

profile of v3, /device:TPU:0, one launch (start us, length us, event | category | flops | bytes accessed | tf_op | source)
XLA Modules:
  0.0 67.1 jit_solution(12387254688238417402)
XLA Ops:
  0.0 1.3 %reshape.23 = f32[2048]{0:T(1024)} convert(bf16[2048]{0:T(1024)(128)(2,1)} %param.10) | non-fusion elementwise | flops 2048 | bytes 12288 | tf_op jit(solution)/shard_map/reshape | solution.py:552
  1.3 1.3 %copy.10.owner_ref = s32[32,1]{1,0:T(8,128)} copy(s32[32,1]{0,1:T(1,128)} %param.12) | data formatting | bytes 256 | tf_op args[3]
  2.6 1.4 %copy.11.table_ref = s32[32,8]{1,0:T(8,128)} copy(s32[32,8]{0,1:T(8,128)} %param.14) | data formatting | bytes 2048 | tf_op args[5]
  4.0 61.4 %shard_map.91 = f32[2,256,128]{2,1,0:T(8,128)} custom-call(bf16[1024,2048]{1,0:T(8,128)(2,1)} %token_ref.1, f32[1,2048]{1,0:T(1,128)} %bitcast.8, bf16[16384,256]{1,0:T(8,128)(2,1)} %bitcast.5, bf16[2,256,128]{2,1,0:T(8,128)(2,1)} %bitcast.7, bf16[2,32,128,256]{3,2,1,0:T(8,128)(2,1)} %cache_ref.1, bf16[2,32,256]{2,1,0:T(8,128)(2,1)} %fresh_ref.1, ...), custom_call_target="tpu_custom_call" | custom-call | tf_op jit(solution)/shard_map/pallas_call | solution.py:507
  65.4 1.7 %copy.13 = f32[2,32,8,128]{3,2,1,0:T(8,128)} copy(f32[2,32,8,128]{3,2,1,0:T(8,128)} %bitcast.6) | data formatting | bytes 524288

commit v4 on v2

--- a/solution.py
+++ b/solution.py
@@ -20,10 +20,10 @@
 def count_pages(
     sections, heads, pool, block, owner_ref, table_ref, length_ref, full_ref, edge_ref, aux_ref
 ):
-    total_blocks = owner_ref.shape[0]
+    total_blocks = owner_ref.shape[1]
     blocks_dev = total_blocks // sections
     slots_peer = 2 * ((blocks_dev + sections - 1) // sections)
-    requests, depth = table_ref.shape
+    depth, requests = table_ref.shape
     cols = full_ref.shape[1]
     me = lax.axis_index("section")
     f32 = jnp.float32
@@ -32,22 +32,19 @@
         return lax.broadcasted_iota(jnp.int32, shape, axis)
 
     grid = (total_blocks, total_blocks)
-    across = jnp.broadcast_to(owner_ref[...], grid)
+    along = jnp.broadcast_to(owner_ref[...], grid).astype(f32)
     row, column = iota(grid, 0), iota(grid, 1)
-    along = jnp.sum(jnp.where(row == column, across, 0).astype(f32), axis=0, keepdims=True)
-    earlier = (across.astype(f32) == along) & (column < row)
+    across = jnp.sum(jnp.where(row == column, along, 0.0), axis=1, keepdims=True)
+    earlier = (across == along) & (column < row)
     earlier = earlier & (lax.div(column, blocks_dev) == lax.div(row, blocks_dev))
     rank = jnp.sum(jnp.where(earlier, 1.0, 0.0), axis=1, keepdims=True)
     tall = (total_blocks, 1)
     slot = pool + lax.div(iota(tall, 0), blocks_dev) * slots_peer
-    placed = jnp.where(owner_ref[...] == me, slot.astype(f32) + rank, -1.0)
+    placed = jnp.where(across == me.astype(f32), slot.astype(f32) + rank, -1.0)
 
     spread = iota((requests, cols), 0) == lax.div(iota((requests, cols), 1), cols // requests)
     spread = jnp.where(spread, 1.0, 0.0)
-    contract = (((0,), (0,)), ((), ()))
-    columns = lax.dot_general(
-        table_ref[...].astype(f32), spread, contract, preferred_element_type=f32
-    )
+    columns = jnp.dot(table_ref[...].astype(f32), spread, preferred_element_type=f32)
     length = jnp.broadcast_to(length_ref[...], (8, requests))
     split = lax.div(length, block)
     blocks_held = jnp.dot(split.astype(f32), spread, preferred_element_type=f32)[:1]
@@ -517,8 +514,8 @@
         decode_query.reshape(heads, cols, dim),
         resident_cache,
         new_kv,
-        block_owner,
-        page_table,
+        block_owner.reshape(1, -1),
+        page_table.T,
         context_len.reshape(1, requests),
     )
     return out.reshape(heads, requests, group_size, dim)

time: 59 us -> 57.5 us (0.975)
  local copies, waits for them, and re-layouts: 2.21 us -> 0.73 us
    unnamed x9 -> x11, local copies, waits for them, and re-layouts: 2.21 us -> 0.73 us
where the time goes in v4:
time: 57.5 us; the launch traced here: 57.3 us
  Pallas kernels  43.2 us (75%)
  matrix products  12.7 us (22%)
  local copies, waits for them, and re-layouts  0.73 us (1%)
  other arithmetic  0.69 us (1%)
    pallas_call x1, Pallas kernels, per_device(): pl.pallas_call(functools.partial(kernel, sections, tp, heads, block, chun...  43.2 us
    dot_general x1, matrix products, per_device(): jnp.einsum('td,dhc->htc', normed, kv_weight, preferred_element_type=jnp.f...  12.7 us

profile of v4, /device:TPU:0, one launch (start us, length us, event | category | flops | bytes accessed | tf_op | source)
XLA Modules:
  0.0 57.3 jit_solution(9093848795984777792)
XLA Ops:
  0.0 0.7 %convert_element_type.15 = f32[2048]{0:T(1024)S(1)} convert(bf16[2048]{0:T(1024)(128)(2,1)} %param.10) | non-fusion elementwise | flops 2048 | bytes 12288 | tf_op jit(solution)/shard_map/convert_element_type | solution.py:461
  0.7 0.0 copy-start
  0.7 0.0 copy-start.1
  0.7 0.0 copy-start.2
  0.7 0.0 copy-start.3
  0.7 0.0 copy-start.4
  0.7 12.7 %convert_bitcast_fusion.part_ref = bf16[8,1024,256]{2,1,0:T(8,128)(2,1)S(1)} fusion(bf16[2048,8,256]{2,1,0:T(8,128)(2,1)} %param.11, bf16[1024,2048]{1,0:T(8,128)(2,1)} %token_ref.1, f32[2048]{0:T(1024)S(1)} %convert_element_type.15), kind=kOutput, calls=%fused_computation.4 | convolution fusion | flops 8598323200 | bytes 16785408 | tf_op jit(solution)/shard_map/td,dhc->htc/dot_general | solution.py:462
  13.4 0.0 copy-done
  13.4 0.0 copy-done.1
  13.4 0.0 copy-done.2
  13.4 0.0 copy-done.3
  13.4 0.0 copy-done.4
  13.4 43.2 %shard_map.91 = f32[2,256,128]{2,1,0:T(8,128)S(1)} custom-call(bf16[8,1024,256]{2,1,0:T(8,128)(2,1)S(1)} %convert_bitcast_fusion.part_ref, bf16[1024,2048]{1,0:T(8,128)(2,1)} %token_ref.1, bf16[2,256,128]{2,1,0:T(8,128)(2,1)S(1)} %bitcast.13, bf16[2,32,128,256]{3,2,1,0:T(8,128)(2,1)} %cache_ref.1, bf16[2,32,256]{2,1,0:T(8,128)(2,1)S(1)} %copy-done.1, ...), custom_call_target="tpu_custom_call" | custom-call | tf_op jit(solution)/shard_map/pallas_call | solution.py:471
  56.6 0.7 %copy.16 = f32[2,32,8,128]{3,2,1,0:T(8,128)} copy(f32[2,32,8,128]{3,2,1,0:T(8,128)S(1)} %bitcast.12) | data formatting | bytes 524288
Async XLA Ops:
  0.7 12.7 %copy-start = (bf16[2,32,8,128]{3,2,1,0:T(8,128)(2,1)S(1)}, bf16[2,32,8,128]{3,2,1,0:T(8,128)(2,1)}, u32[]{:S(2)}) copy-start(bf16[2,32,8,128]{3,2,1,0:T(8,128)(2,1)} %param.16) | copy-start | bytes 393220
  0.7 12.7 %copy-start.1 = (bf16[2,32,256]{2,1,0:T(8,128)(2,1)S(1)}, bf16[2,32,256]{2,1,0:T(8,128)(2,1)}, u32[]{:S(2)}) copy-start(bf16[2,32,256]{2,1,0:T(8,128)(2,1)} %fresh_ref.1) | copy-start | bytes 98308
  0.7 12.7 %copy-start.2 = (s32[32,8]{0,1:T(8,128)S(1)}, s32[32,8]{0,1:T(8,128)}, u32[]{:S(2)}) copy-start(s32[32,8]{0,1:T(8,128)} %param.14) | copy-start | bytes 3076
  0.7 12.7 %copy-start.3 = (s32[32,1]{0,1:T(1,128)S(1)}, s32[32,1]{0,1:T(1,128)}, u32[]{:S(2)}) copy-start(s32[32,1]{0,1:T(1,128)} %param.12) | copy-start | bytes 388
  0.7 12.7 %copy-start.4 = (s32[32]{0:T(128)S(1)}, s32[32]{0:T(128)}, u32[]{:S(2)}) copy-start(s32[32]{0:T(128)} %param.15) | copy-start | bytes 388

commit v5 on v4

--- a/solution.py
+++ b/solution.py
@@ -457,8 +457,7 @@
     chunk = min(rows, 512)
     chunks = rows // chunk
     chips = tp // 2
-    widened = tokens.astype(jnp.float32)
-    normed = (widened * norm_gain.astype(jnp.float32)[None, :]).astype(jnp.bfloat16)
+    normed = tokens * norm_gain[None, :]
     part = jnp.einsum(
         "td,dhc->htc", normed, kv_weight, preferred_element_type=jnp.float32
     ).astype(jnp.bfloat16)

time: 57.5 us -> 56.8 us (0.988)
  other arithmetic: 0.69 us -> 0 us
    convert_element_type x1 -> x0, other arithmetic: 0.69 us -> none  [per_device(): norm_gain.astype(jnp.float32)[None, :]]
where the time goes in v5:
time: 56.8 us; the launch traced here: 56.6 us
  Pallas kernels  43.2 us (76%)
  matrix products  12.7 us (22%)
  local copies, waits for them, and re-layouts  0.72 us (1%)
    pallas_call x1, Pallas kernels, per_device(): pl.pallas_call(functools.partial(kernel, sections, tp, heads, block, chun...  43.2 us
    dot_general x1, matrix products, per_device(): jnp.einsum('td,dhc->htc', normed, kv_weight, preferred_element_type=jnp.f...  12.7 us

profile of v5, /device:TPU:0, one launch (start us, length us, event | category | flops | bytes accessed | tf_op | source)
XLA Modules:
  0.0 56.6 jit_solution(7663160728692344884)
XLA Ops:
  0.0 0.0 copy-start
  0.0 0.0 copy-start.1
  0.0 0.0 copy-start.2
  0.0 0.0 copy-start.3
  0.0 0.0 copy-start.4
  0.0 12.7 %convert_bitcast_fusion.part_ref = bf16[8,1024,256]{2,1,0:T(8,128)(2,1)S(1)} fusion(bf16[2048,8,256]{2,1,0:T(8,128)(2,1)} %param.11, bf16[1024,2048]{1,0:T(8,128)(2,1)} %token_ref.1, bf16[2048]{0:T(1024)(128)(2,1)} %param.10), kind=kOutput, calls=%fused_computation.3 | convolution fusion | flops 8600420352 | bytes 16781312 | tf_op jit(solution)/shard_map/td,dhc->htc/dot_general | solution.py:461
  12.7 0.0 copy-done
  12.7 0.0 copy-done.1
  12.7 0.0 copy-done.2
  12.7 0.0 copy-done.3
  12.7 0.0 copy-done.4
  12.7 43.2 %shard_map.91 = f32[2,256,128]{2,1,0:T(8,128)S(1)} custom-call(bf16[8,1024,256]{2,1,0:T(8,128)(2,1)S(1)} %convert_bitcast_fusion.part_ref, bf16[1024,2048]{1,0:T(8,128)(2,1)} %token_ref.1, bf16[2,256,128]{2,1,0:T(8,128)(2,1)S(1)} %bitcast.13, bf16[2,32,128,256]{3,2,1,0:T(8,128)(2,1)} %cache_ref.1, bf16[2,32,256]{2,1,0:T(8,128)(2,1)S(1)} %copy-done.1, ...), custom_call_target="tpu_custom_call" | custom-call | tf_op jit(solution)/shard_map/pallas_call | solution.py:470
  55.9 0.7 %copy.16 = f32[2,32,8,128]{3,2,1,0:T(8,128)} copy(f32[2,32,8,128]{3,2,1,0:T(8,128)S(1)} %bitcast.12) | data formatting | bytes 524288
Async XLA Ops:
  0.0 12.7 %copy-start = (bf16[2,32,8,128]{3,2,1,0:T(8,128)(2,1)S(1)}, bf16[2,32,8,128]{3,2,1,0:T(8,128)(2,1)}, u32[]{:S(2)}) copy-start(bf16[2,32,8,128]{3,2,1,0:T(8,128)(2,1)} %param.16) | copy-start | bytes 393220
  0.0 12.7 %copy-start.1 = (bf16[2,32,256]{2,1,0:T(8,128)(2,1)S(1)}, bf16[2,32,256]{2,1,0:T(8,128)(2,1)}, u32[]{:S(2)}) copy-start(bf16[2,32,256]{2,1,0:T(8,128)(2,1)} %fresh_ref.1) | copy-start | bytes 98308
  0.0 12.7 %copy-start.2 = (s32[32,8]{0,1:T(8,128)S(1)}, s32[32,8]{0,1:T(8,128)}, u32[]{:S(2)}) copy-start(s32[32,8]{0,1:T(8,128)} %param.14) | copy-start | bytes 3076
  0.0 12.7 %copy-start.3 = (s32[32,1]{0,1:T(1,128)S(1)}, s32[32,1]{0,1:T(1,128)}, u32[]{:S(2)}) copy-start(s32[32,1]{0,1:T(1,128)} %param.12) | copy-start | bytes 388
  0.0 12.7 %copy-start.4 = (s32[32]{0:T(128)S(1)}, s32[32]{0:T(128)}, u32[]{:S(2)}) copy-start(s32[32]{0:T(128)} %param.15) | copy-start | bytes 388
